TPU v7x, 128 devices: a whole 4x4x4 slice. The times are simulated.
128 devices in a mesh: seq: 16 (over z, y_hi, core), blk: 8 (over y_lo, x).
Axes of the slice: x: 4, y: 4 (y_hi: 2, y_lo: 2; y = y_hi * 2 + y_lo), z: 4, core: 2. Of those that a mesh axis runs over, the one named last changes fastest.
Arguments:
- tokens: bfloat16 [16384, 8192], P('seq', 'blk'), may hold values from -6 to 6
- right_factor: bfloat16 [64, 128, 128], P('blk', 'seq'), may hold values from -0.5 to 0.5
- left_factor: bfloat16 [128, 64, 64], P('blk', 'seq'), may hold values from -0.75 to 0.75
- target: bfloat16 [16384, 8192], P('seq', 'blk'), may hold values from -4 to 4
Outputs:
- student: bfloat16 [16384, 8192], P('seq', 'blk')
- right_grad: float32 [64, 128, 128], P('blk', 'seq')
- left_grad: float32 [128, 64, 64], P('blk', 'seq')
All inputs are finite; a program needn't handle non-finite values.
Results may differ from a plain program's by a relative error of at most 0.017.
Values may be sent and summed in bfloat16 or wider, within the bound.
No kernel may reach another device: no remote copies, remote signals or barrier semaphores. Data moves between devices by JAX's collectives and lax.ppermute only.
A program may use at most 64 MiB of HBM per device.

v0:
```python
import jax
import jax.numpy as jnp
from jax import lax
from jax.sharding import PartitionSpec as P


def gelu_tanh(values):
    return jax.nn.gelu(values, approximate=True)


def shards(tokens, right_factor, left_factor, target):
    rows = tokens.shape[0]
    count = rows * lax.axis_size("seq")
    scale = 1.0 / jnp.sqrt(jnp.float32(count))
    right_full, left_full = (
        lax.all_gather(right_factor, "seq", axis=1, tiled=True),
        lax.all_gather(left_factor, "seq", axis=1, tiled=True),
    )
    nblocks = left_full.shape[1]
    local_blocks = right_full.shape[0]
    width = right_full.shape[1]
    inputs = tokens.reshape(rows, local_blocks, width)
    mixed = jnp.einsum(
        "tki,kci->tkc", inputs, right_full, preferred_element_type=jnp.float32
    ).astype(jnp.bfloat16)
    turned = lax.all_to_all(mixed, "blk", split_axis=2, concat_axis=1, tiled=True)
    turned, pre = (
        turned,
        jnp.einsum("tkc,cmk->tcm", turned, left_full, preferred_element_type=jnp.float32),
    )
    local_cols = pre.shape[1]
    act, back = jax.vjp(gelu_tanh, pre)
    student = act.reshape(rows, local_cols * nblocks).astype(jnp.bfloat16)
    residual = (act - target.reshape(rows, local_cols, nblocks).astype(jnp.float32)) * scale
    pre_grad = back(residual)[0].astype(jnp.bfloat16)
    turned_grad = jnp.einsum(
        "tcm,cmk->tkc", pre_grad, left_full, preferred_element_type=jnp.float32
    ).astype(jnp.bfloat16)
    mixed_grad = lax.all_to_all(turned_grad, "blk", split_axis=1, concat_axis=2, tiled=True)
    left_term = jnp.einsum("tcm,tkc->cmk", pre_grad, turned, preferred_element_type=jnp.float32)
    right_term = jnp.einsum("tkc,tki->kci", mixed_grad, inputs, preferred_element_type=jnp.float32)
    right_total, left_total = (
        lax.psum(right_term.astype(jnp.bfloat16), "seq").astype(jnp.float32),
        lax.psum(left_term.astype(jnp.bfloat16), "seq").astype(jnp.float32),
    )
    place = lax.axis_index("seq")
    right_rows = right_factor.shape[1]
    left_rows = left_factor.shape[1]
    right_grad = lax.dynamic_slice_in_dim(right_total, place * right_rows, right_rows, 1)
    left_grad = lax.dynamic_slice_in_dim(left_total, place * left_rows, left_rows, 1)
    return (student, right_grad, left_grad)


def solution(mesh):
    return jax.shard_map(
        shards,
        mesh=mesh,
        in_specs=(P("seq", "blk"), P("blk", "seq", None), P("blk", "seq", None), P("seq", "blk")),
        out_specs=(P("seq", "blk"), P("blk", "seq", None), P("blk", "seq", None)),
        check_vma=False,
    )
```

profile of v0, /device:TPU:1, one launch (start us, length us, event | category | flops | bytes accessed | tf_op | source)
XLA Modules:
  0.0 280.4 jit_solution(13000971417474091226)
XLA Ops:
  7.2 0.0 copy-start
  7.2 28.3 %all_gather.6 = bf16[8,128,128]{2,1,0:T(8,128)(2,1)S(1)} all-gather(bf16[8,8,128]{2,1,0:T(8,128)(2,1)} %param.5), channel_id=1, replica_groups=mesh['seq'=16,'blk'=8] {'seq'}, dimensions={1}, use_global_device_ids=true | all-gather | bytes 278528 | tf_op jit(solution)/shard_map/all_gather | solution.py:16
  35.5 0.7 convert_bitcast_fusion.1
  36.3 2.5 copy.14
  38.7 4.5 %all-to-all-start = ((bf16[1024,8,128]{0,1,2:T(8,128)(2,1)}), bf16[1024,8,128]{0,1,2:T(8,128)(2,1)}, u32[]{:S(2)}, u32[]{:S(2)}) async-start(bf16[1024,8,128]{0,1,2:T(8,128)(2,1)} %copy.14), calls=%async_computation | async-start | bytes 4194304 | tf_op jit(solution)/shard_map/all_to_all | solution.py:26
  43.2 0.0 copy-done.2
  43.2 4.1 %copy.18 = f32[1024,1024]{0,1:T(8,128)} copy(bf16[1024,1024]{1,0:T(8,128)(2,1)} %param.7) | data formatting | bytes 6291456 | tf_op jit(solution)/shard_map/convert_element_type | solution.py:34
  47.4 31.7 %all_gather.7 = bf16[16,64,64]{2,0,1:T(8,128)(2,1)S(1)} all-gather(bf16[16,4,64]{2,0,1:T(8,128)(2,1)S(1)} %copy.16), channel_id=1, replica_groups=mesh['seq'=16,'blk'=8] {'seq'}, dimensions={1}, use_global_device_ids=true | all-gather | bytes 139264 | tf_op jit(solution)/shard_map/all_gather | solution.py:17
  79.1 0.0 all-to-all-done
  79.1 7.1 %fusion.6 = (bf16[1024,16,64]{0,2,1:T(8,128)(2,1)S(1)}, bf16[1024,16,64]{0,2,1:T(8,128)(2,1)}) fusion(f32[1024,16,64]{0,2,1:T(8,128)} %bitcast.61, bf16[1024,8,8,16]{0,1,3,2:T(8,128)(2,1)} %bitcast.1, bf16[16,64,64]{2,0,1:T(8,128)(2,1)S(1)} %all_gather.7), kind=kOutput, calls=%fused_computation.8 | convolution fusion | flops 159383552 | bytes 10616832 | tf_op jit(solution)/shard_map/tkc,cmk->tcm/dot_general | solution.py:29
  86.2 0.8 convert_bitcast_fusion
  87.0 0.6 copy-done.1
  87.5 2.5 copy.20
  90.0 11.2 %all-to-all-start.1 = ((bf16[1024,64,16]{0,2,1:T(8,128)(2,1)}), bf16[1024,64,16]{0,2,1:T(8,128)(2,1)}, u32[]{:S(2)}, u32[]{:S(2)}) async-start(bf16[1024,64,16]{0,2,1:T(8,128)(2,1)} %copy.20), calls=%async_computation.1 | async-start | bytes 4194304 | tf_op jit(solution)/shard_map/all_to_all | solution.py:39
  101.2 0.0 all-reduce.3.cloned.1.call-start
  101.3 3.7 %fusion.24 = bf16[16,64,64]{2,1,0:T(8,128)(2,1)} fusion(bf16[1024,16,64]{0,2,1:T(8,128)(2,1)} %copy-done.1, bf16[1024,8,8,16]{0,1,3,2:T(8,128)(2,1)} %bitcast.1), kind=kOutput, calls=%fused_computation.28 | convolution fusion | flops 134283264 | bytes 4325376 | tf_op jit(solution)/shard_map/tcm,tkc->cmk/dot_general | solution.py:40
  104.9 23.5 %all-to-all-done.1 = bf16[1024,64,16]{0,2,1:T(8,128)(2,1)} async-done(((bf16[1024,64,16]{0,2,1:T(8,128)(2,1)}), bf16[1024,64,16]{0,2,1:T(8,128)(2,1)}, u32[]{:S(2)}, u32[]{:S(2)}) %all-to-all-start.1) | async-done | bytes 2097184 | tf_op jit(solution)/shard_map/all_to_all | solution.py:39
  128.4 1.8 copy.21
  130.2 1.5 fusion.27
  131.7 0.0 all-reduce.3.cloned.1.call-update
  131.8 3.9 %copy.23 = bf16[1024,1024]{1,0:T(8,128)(2,1)} copy(bf16[1024,1024]{0,1:T(8,128)(2,1)} %bitcast.62) | data formatting | bytes 4194304
  135.7 135.1 %all-reduce.3.cloned.1.call-done = (bf16[8,128,128]{2,1,0:T(8,128)(2,1)}, bf16[16,64,64]{2,1,0:T(8,128)(2,1)}) async-done(((bf16[8,128,128]{2,1,0:T(8,128)(2,1)}, bf16[16,64,64]{2,1,0:T(8,128)(2,1)}), (bf16[8,128,128]{2,1,0:T(8,128)(2,1)}, bf16[16,64,64]{2,1,0:T(8,128)(2,1)})) %all-reduce.3.cloned.1.call-update) | async-done | bytes 393232 | tf_op jit(solution)/shard_map/psum | solution.py:43
  270.8 1.4 dynamic-slice_convert_fusion
  272.2 1.3 dynamic-slice_convert_fusion.1
  (4 shorter events, 0.0 us)
Async XLA Ops:
  7.2 28.4 %copy-start = (bf16[1024,1024]{1,0:T(8,128)(2,1)S(1)}, bf16[1024,1024]{1,0:T(8,128)(2,1)}, u32[]{:S(2)}) copy-start(bf16[1024,1024]{1,0:T(8,128)(2,1)} %param.4) | copy-start | bytes 6291460
  38.7 4.5 %copy-start.2 = (bf16[16,4,64]{2,1,0:T(4,128)(2,1)S(1)}, bf16[16,4,64]{2,1,0:T(4,128)(2,1)}, u32[]{:S(2)}) copy-start(bf16[16,4,64]{2,1,0:T(4,128)(2,1)} %param.6) | copy-start | bytes 24580
  38.7 40.4 %all-to-all-start = ((bf16[1024,8,128]{0,1,2:T(8,128)(2,1)}), bf16[1024,8,128]{0,1,2:T(8,128)(2,1)}, u32[]{:S(2)}, u32[]{:S(2)}) async-start(bf16[1024,8,128]{0,1,2:T(8,128)(2,1)} %copy.14), calls=%async_computation | async-start | bytes 4194304 | tf_op jit(solution)/shard_map/all_to_all | solution.py:26
  86.2 1.3 copy-start.1
  90.0 38.4 %all-to-all-start.1 = ((bf16[1024,64,16]{0,2,1:T(8,128)(2,1)}), bf16[1024,64,16]{0,2,1:T(8,128)(2,1)}, u32[]{:S(2)}, u32[]{:S(2)}) async-start(bf16[1024,64,16]{0,2,1:T(8,128)(2,1)} %copy.20), calls=%async_computation.1 | async-start | bytes 4194304 | tf_op jit(solution)/shard_map/all_to_all | solution.py:39
  101.2 169.6 %all-reduce.3.cloned.1.call-start = ((), (), s32[]{:S(2)}) async-start(), calls=%async_computation.2 | async-start | bytes 1048576 | tf_op jit(solution)/shard_map/psum | solution.py:43
Sparse Core Ops, SparseCore 0:
  131.9 138.8 all-reduce.2
where the time goes:
time: 281 us; the launch traced here: 280 us
  waiting for transfers between devices  159 us (57%)
  blocking collectives  60.1 us (21%)
  starting transfers between devices  15.7 us (6%)
  local copies, waits for them, and re-layouts  15.4 us (5%)
  between operations  14.1 us (5%)
  matrix products  13.8 us (5%)
    psum x1, waiting for transfers between devices, shards(): lax.psum(right_term.astype(jnp.bfloat16), 'seq').astype(jnp.float32)  135 us
    all_gather x1, blocking collectives, shards(): lax.all_gather(left_factor, 'seq', axis=1, tiled=True)  31.7 us
    all_gather x1, blocking collectives, shards(): lax.all_gather(right_factor, 'seq', axis=1, tiled=True)  28.3 us
    all_to_all x1, waiting for transfers between devices, shards(): lax.all_to_all(turned_grad, 'blk', split_axis=1, concat_axis=2, tiled=True)  23.5 us
    all_to_all x1, starting transfers between devices, shards(): lax.all_to_all(turned_grad, 'blk', split_axis=1, concat_axis=2, tiled=True)  11.2 us
    dot_general x1, matrix products, shards(): jnp.einsum('tkc,cmk->tcm', turned, left_full, preferred_element_type=jnp....  7.07 us
  transfers between devices with their start and end apart: 3, of which 2 were waited for; matrix products, arithmetic and copies ran while one was open for 4% of the time, Pallas kernels for 0%

commit v1 on v0

--- a/solution.py
+++ b/solution.py
@@ -2,6 +2,11 @@
 import jax.numpy as jnp
 from jax import lax
 from jax.sharding import PartitionSpec as P
+
+
+def gather_over(x, axis, dim):
+    stack = jnp.stack([x] * lax.axis_size(axis))
+    return jnp.concatenate(lax.all_to_all(stack, axis, 0, 0), axis=dim)
 
 
 def gelu_tanh(values):
@@ -13,7 +18,7 @@
     count = rows * lax.axis_size("seq")
     scale = 1.0 / jnp.sqrt(jnp.float32(count))
     right_full, left_full = (
-        lax.all_gather(right_factor, "seq", axis=1, tiled=True),
+        gather_over(right_factor, "seq", 1),
         lax.all_gather(left_factor, "seq", axis=1, tiled=True),
     )
     nblocks = left_full.shape[1]

time: 281 us -> 271 us (0.964)
  blocking collectives: 60.1 us -> 52.4 us
    all_gather x1 -> x0, blocking collectives: 28.3 us -> none  [shards(): lax.all_gather(right_factor, 'seq', axis=1, tiled=True)]
    all_to_all x0 -> x1, blocking collectives: none -> 17.9 us  [gather_over(): return jnp.concatenate(lax.all_to_all(stack, axis, 0, 0), axis=dim)]
    all_to_all x1, starting transfers between devices: 11.2 us -> 8.37 us  [shards(): lax.all_to_all(turned_grad, 'blk', split_axis=1, concat_axis=2, tiled=True)]
where the time goes in v1:
time: 271 us
  waiting for transfers between devices  158 us (58%)
  blocking collectives  52.4 us (19%)
  local copies, waits for them, and re-layouts  16.3 us (6%)
  between operations  14.1 us (5%)
  matrix products  13.8 us (5%)
  starting transfers between devices  12.9 us (5%)
  other arithmetic  2.71 us (1%)
    psum x1, waiting for transfers between devices, shards(): lax.psum(right_term.astype(jnp.bfloat16), 'seq').astype(jnp.float32)  135 us
    all_gather x1, blocking collectives, shards(): lax.all_gather(left_factor, 'seq', axis=1, tiled=True)  34.5 us
    all_to_all x1, waiting for transfers between devices, shards(): lax.all_to_all(turned_grad, 'blk', split_axis=1, concat_axis=2, tiled=True)  23.5 us
    all_to_all x1, blocking collectives, gather_over(): return jnp.concatenate(lax.all_to_all(stack, axis, 0, 0), axis=dim)  17.9 us
    all_to_all x1, starting transfers between devices, shards(): lax.all_to_all(turned_grad, 'blk', split_axis=1, concat_axis=2, tiled=True)  8.37 us
    dot_general x1, matrix products, shards(): jnp.einsum('tkc,cmk->tcm', turned, left_full, preferred_element_type=jnp....  7.07 us
  transfers between devices with their start and end apart: 3, of which 2 were waited for; matrix products, arithmetic and copies ran while one was open for 4% of the time, Pallas kernels for 0%

profile of v1, /device:TPU:1, one launch (start us, length us, event | category | flops | bytes accessed | tf_op | source)
XLA Modules:
  0.0 270.7 jit_solution(14488494304396283827)
XLA Ops:
  7.2 0.0 copy-start
  7.2 0.9 stack.2
  8.1 17.9 %all_to_all.41 = bf16[16,8,8,128]{3,2,1,0:T(8,128)(2,1)S(1)} all-to-all(bf16[16,8,8,128]{3,2,1,0:T(8,128)(2,1)S(1)} %stack.2), channel_id=1, replica_groups=mesh['seq'=16,'blk'=8] {'seq'}, dimensions={0} | all-to-all | bytes 524288 | tf_op jit(solution)/shard_map/all_to_all | solution.py:9
  26.0 0.7 convert_bitcast_fusion.1
  26.8 2.5 copy.15
  29.2 4.5 %all-to-all-start.1 = ((bf16[1024,8,128]{0,1,2:T(8,128)(2,1)}), bf16[1024,8,128]{0,1,2:T(8,128)(2,1)}, u32[]{:S(2)}, u32[]{:S(2)}) async-start(bf16[1024,8,128]{0,1,2:T(8,128)(2,1)} %copy.15), calls=%async_computation.1 | async-start | bytes 4194304 | tf_op jit(solution)/shard_map/all_to_all | solution.py:31
  33.8 4.1 %copy.19 = f32[1024,1024]{0,1:T(8,128)} copy(bf16[1024,1024]{1,0:T(8,128)(2,1)} %param.7) | data formatting | bytes 6291456 | tf_op jit(solution)/shard_map/convert_element_type | solution.py:39
  37.9 34.5 %all_gather.3 = bf16[16,64,64]{2,0,1:T(8,128)(2,1)S(1)} all-gather(bf16[16,4,64]{2,0,1:T(8,128)(2,1)S(1)} %copy.17), channel_id=1, replica_groups=mesh['seq'=16,'blk'=8] {'seq'}, dimensions={1}, use_global_device_ids=true | all-gather | bytes 139264 | tf_op jit(solution)/shard_map/all_gather | solution.py:22
  72.4 0.0 all-to-all-done.1
  72.4 7.1 %fusion.6 = (bf16[1024,16,64]{0,2,1:T(8,128)(2,1)S(1)}, bf16[1024,16,64]{0,2,1:T(8,128)(2,1)}) fusion(f32[1024,16,64]{0,2,1:T(8,128)} %bitcast.67, bf16[1024,8,8,16]{0,1,3,2:T(8,128)(2,1)} %bitcast.3, bf16[16,64,64]{2,0,1:T(8,128)(2,1)S(1)} %all_gather.3), kind=kOutput, calls=%fused_computation.8 | convolution fusion | flops 159383552 | bytes 10616832 | tf_op jit(solution)/shard_map/tkc,cmk->tcm/dot_general | solution.py:34
  79.5 0.8 convert_bitcast_fusion
  80.2 0.6 copy-done.1
  80.8 2.5 copy.21
  83.3 8.4 %all-to-all-start.2 = ((bf16[1024,64,16]{0,2,1:T(8,128)(2,1)}), bf16[1024,64,16]{0,2,1:T(8,128)(2,1)}, u32[]{:S(2)}, u32[]{:S(2)}) async-start(bf16[1024,64,16]{0,2,1:T(8,128)(2,1)} %copy.21), calls=%async_computation.2 | async-start | bytes 4194304 | tf_op jit(solution)/shard_map/all_to_all | solution.py:44
  91.6 0.0 all-reduce.3.cloned.1.call-start
  91.7 3.7 %fusion.24 = bf16[16,64,64]{2,1,0:T(8,128)(2,1)} fusion(bf16[1024,16,64]{0,2,1:T(8,128)(2,1)} %copy-done.1, bf16[1024,8,8,16]{0,1,3,2:T(8,128)(2,1)} %bitcast.3), kind=kOutput, calls=%fused_computation.28 | convolution fusion | flops 134283264 | bytes 4325376 | tf_op jit(solution)/shard_map/tcm,tkc->cmk/dot_general | solution.py:45
  95.4 23.5 %all-to-all-done.2 = bf16[1024,64,16]{0,2,1:T(8,128)(2,1)} async-done(((bf16[1024,64,16]{0,2,1:T(8,128)(2,1)}), bf16[1024,64,16]{0,2,1:T(8,128)(2,1)}, u32[]{:S(2)}, u32[]{:S(2)}) %all-to-all-start.2) | async-done | bytes 2097184 | tf_op jit(solution)/shard_map/all_to_all | solution.py:44
  118.9 1.8 copy.22
  120.6 1.5 fusion.27
  122.2 0.0 all-reduce.3.cloned.1.call-update
  122.2 3.9 %copy.24 = bf16[1024,1024]{1,0:T(8,128)(2,1)} copy(bf16[1024,1024]{0,1:T(8,128)(2,1)} %bitcast.68) | data formatting | bytes 4194304
  126.1 135.0 %all-reduce.3.cloned.1.call-done = (bf16[8,128,128]{2,1,0:T(8,128)(2,1)}, bf16[16,64,64]{2,1,0:T(8,128)(2,1)}) async-done(((bf16[8,128,128]{2,1,0:T(8,128)(2,1)}, bf16[16,64,64]{2,1,0:T(8,128)(2,1)}), (bf16[8,128,128]{2,1,0:T(8,128)(2,1)}, bf16[16,64,64]{2,1,0:T(8,128)(2,1)})) %all-reduce.3.cloned.1.call-update) | async-done | bytes 393232 | tf_op jit(solution)/shard_map/psum | solution.py:48
  261.1 1.4 dynamic-slice_convert_fusion
  262.5 1.3 dynamic-slice_convert_fusion.1
  (5 shorter events, 0.0 us)
Async XLA Ops:
  7.2 18.9 %copy-start = (bf16[1024,1024]{1,0:T(8,128)(2,1)S(1)}, bf16[1024,1024]{1,0:T(8,128)(2,1)}, u32[]{:S(2)}) copy-start(bf16[1024,1024]{1,0:T(8,128)(2,1)} %param.4) | copy-start | bytes 6291460
  29.2 4.5 %copy-start.2 = (bf16[16,4,64]{2,1,0:T(4,128)(2,1)S(1)}, bf16[16,4,64]{2,1,0:T(4,128)(2,1)}, u32[]{:S(2)}) copy-start(bf16[16,4,64]{2,1,0:T(4,128)(2,1)} %param.6) | copy-start | bytes 24580
  29.2 43.2 %all-to-all-start.1 = ((bf16[1024,8,128]{0,1,2:T(8,128)(2,1)}), bf16[1024,8,128]{0,1,2:T(8,128)(2,1)}, u32[]{:S(2)}, u32[]{:S(2)}) async-start(bf16[1024,8,128]{0,1,2:T(8,128)(2,1)} %copy.15), calls=%async_computation.1 | async-start | bytes 4194304 | tf_op jit(solution)/shard_map/all_to_all | solution.py:31
  79.5 1.3 copy-start.1
  83.3 35.6 %all-to-all-start.2 = ((bf16[1024,64,16]{0,2,1:T(8,128)(2,1)}), bf16[1024,64,16]{0,2,1:T(8,128)(2,1)}, u32[]{:S(2)}, u32[]{:S(2)}) async-start(bf16[1024,64,16]{0,2,1:T(8,128)(2,1)} %copy.21), calls=%async_computation.2 | async-start | bytes 4194304 | tf_op jit(solution)/shard_map/all_to_all | solution.py:44
  91.6 169.5 %all-reduce.3.cloned.1.call-start = ((), (), s32[]{:S(2)}) async-start(), calls=%async_computation.3 | async-start | bytes 1048576 | tf_op jit(solution)/shard_map/psum | solution.py:48
Sparse Core Ops, SparseCore 0:
  122.3 138.7 all-reduce.2
